TPU v7x, 32 devices: a whole 2x2x4 slice. The times are simulated.
32 devices in a mesh: blocks: 2 (over y), space: 4 (over z), tm: 2 (over x), span: 2 (over core).
Axes of the slice: x: 2, y: 2, z: 4, core: 2. Of those that a mesh axis runs over, the one named last changes fastest.
Arguments:
- snapshots: float32 [320, 64, 512], P(('blocks', 'tm'), 'space', 'span'), parts along dimension 0, may hold values from -6 to 6
- lagrange_weights: float32 [512, 6], P(('blocks', 'tm')), parts along dimension 0, may hold values from -3 to 3
- source_start: int32 [512], P(('blocks', 'tm')), parts along dimension 0, may hold values from 0 to 156
- band_len: int32 [512], P(('blocks', 'tm')), parts along dimension 0, may hold values from 4 to 6
- band_list: int32 [8], replicated, may hold values from 0 to 15, as said below
- row_metric: float32 [64], P('space'), may hold values from 0.5 to 2
Outputs:
- spectra: float32 [256, 2, 64, 512], P(('blocks', 'space', 'tm'), None, None, 'span'), parts along dimension 0
There are 2 independent parts, one for each index of `blocks`. A program takes and returns all parts, laid end to end along the dimension named above; an argument that names none is the same for every part. Nothing has to cross between parts.
Inputs may be any that keep to these rules, and one draw needn't show every extreme that they name: `band_list`: 8 distinct band numbers.
All inputs are finite; a program needn't handle non-finite values.
Results may differ from a plain program's by a relative error of at most 0.0001.
Values sent between devices are 32-bit elements; how exact they have to be, the bound alone decides.
A program may use at most 64 MiB of HBM per device.

v0:
```python
import math
import jax
import jax.numpy as jnp
from jax import lax
from jax.sharding import PartitionSpec as P

HALO = 16
NT = 256
BW = 8
NL = 8


def extended(cells, sides, width, closed):
    for axis, dim in sides:
        count = lax.axis_size(axis)
        ends = count if closed else count - 1
        head = lax.slice_in_dim(cells, 0, width, axis=dim)
        tail = lax.slice_in_dim(cells, cells.shape[dim] - width, cells.shape[dim], axis=dim)
        cells = jnp.concatenate(
            [
                lax.ppermute(tail, axis, [(i, (i + 1) % count) for i in range(ends)]),
                cells,
                lax.ppermute(head, axis, [((i + 1) % count, i) for i in range(ends)]),
            ],
            axis=dim,
        )
    return cells


def dft_rows(band_list, row_ids, first_sample, count):
    listed_idx = row_ids // 2
    is_imag = row_ids % 2
    band_pos = listed_idx // BW
    matches = band_pos[:, None] == jnp.arange(band_list.shape[0])[None, :]
    band_of = jnp.sum(jnp.where(matches, band_list[None, :], 0), axis=1)
    frequency = band_of * BW + listed_idx % BW
    sample_ids = first_sample + jnp.arange(count)
    phase_idx = frequency[:, None] * sample_ids[None, :] % NT
    angles = 2.0 * math.pi / NT * phase_idx.astype(jnp.float32)
    window = 0.5 - 0.5 * jnp.cos(2.0 * math.pi / NT * sample_ids.astype(jnp.float32))
    weighting = window / math.sqrt(NT)
    waves = jnp.where(is_imag[:, None] == 0, jnp.cos(angles), -jnp.sin(angles))
    return waves * weighting[None, :]


def shards(snapshots, lagrange_weights, source_start, band_len, band_list, row_metric):
    tm_index = lax.axis_index("tm")
    n_tm, n_space = (lax.axis_size("tm"), lax.axis_size("space"))
    steps_dev, rows_dev, span_cells = snapshots.shape
    samples = source_start.shape[0]
    reach = extended(snapshots, (("tm", 0),), HALO, False)
    reach_len = steps_dev + 2 * HALO
    anchor = tm_index * steps_dev - HALO
    slot_ids = jnp.arange(6)
    columns = source_start[:, None] + slot_ids[None, :] - anchor
    active = slot_ids[None, :] < band_len[:, None]
    selected = (columns[:, :, None] == jnp.arange(reach_len)[None, None, :]) & active[:, :, None]
    interp_matrix = jnp.sum(
        jnp.where(selected, lagrange_weights[:, :, None], jnp.float32(0.0)), axis=1
    )
    total_rows = 2 * NL * BW
    own = total_rows // (n_tm * n_space)
    positions = jnp.arange(total_rows).reshape(n_space, n_tm, own).transpose(1, 0, 2).reshape(-1)
    coeffs = dft_rows(band_list, positions, tm_index * samples, samples)
    combined = jnp.dot(coeffs, interp_matrix, precision=lax.Precision.HIGHEST)
    partial = jnp.dot(
        combined, reach.reshape(reach_len, rows_dev * span_cells), precision=lax.Precision.HIGHEST
    )
    summed = lax.psum_scatter(partial, "tm", scatter_dimension=0, tiled=True)
    summed = summed.reshape(n_space * own, rows_dev, span_cells)
    fields = lax.all_to_all(summed, "space", split_axis=0, concat_axis=1, tiled=True)
    metric = lax.all_gather(row_metric, "space", tiled=True)
    row_padded = jnp.pad(fields, ((0, 0), (1, 1), (0, 0)))
    along_rows = 0.5 * metric[None, :, None] * (row_padded[:, 2:, :] - row_padded[:, :-2, :])
    span_padded = extended(fields, (("span", 2),), 1, True)
    along_span = 0.5 * (span_padded[:, :, 2:] - span_padded[:, :, :-2])
    return jnp.stack((along_rows, along_span), axis=1)


def solution(mesh):
    placed = (
        P(("blocks", "tm"), "space", "span"),
        P(("blocks", "tm"), None),
        P(("blocks", "tm")),
        P(("blocks", "tm")),
        P(),
        P("space"),
    )
    return jax.shard_map(
        shards,
        mesh=mesh,
        in_specs=placed,
        out_specs=P(("blocks", "space", "tm"), None, None, "span"),
        check_vma=False,
    )
```

profile of v0, /device:TPU:0, one launch (start us, length us, event | category | flops | bytes accessed | tf_op | source)
XLA Modules:
  0.0 104.5 jit_solution(15764756894311047526)
XLA Ops:
  6.5 0.0 copy-start
  6.5 0.0 reduce-scatter.2.cloned.1.call-start
  6.5 1.2 %fusion.34 = (f32[16,16,256]{2,1,0:T(8,128)S(1)}, f32[16,16,256]{2,1,0:T(8,128)S(1)}) fusion(f32[80,16,256]{2,1,0:T(8,128)} %param.6), kind=kLoop, calls=%fused_computation.64 | loop fusion | bytes 1048576 | tf_op jit(solution)/shard_map/slice | solution.py:18
  7.7 4.9 %collective-permute-start = (f32[16,16,256]{2,1,0:T(8,128)S(1)}, f32[16,16,256]{2,1,0:T(8,128)S(1)}, u32[]{:S(2)}, u32[]{:S(2)}) collective-permute-start(f32[16,16,256]{2,1,0:T(8,128)S(1)} %get-tuple-element.7), channel_id=1, source_target_pairs={{0,2},{1,3},{4,6},{5,7},{8,10},{9,11},{12,14},{13,15},{16,18},{17,... | collective-permute-start | bytes 786440 | tf_op jit(solution)/shard_map/ppermute | solution.py:21
  12.6 1.3 %collective-permute-start.1 = (f32[16,16,256]{2,1,0:T(8,128)S(1)}, f32[16,16,256]{2,1,0:T(8,128)S(1)}, u32[]{:S(2)}, u32[]{:S(2)}) collective-permute-start(f32[16,16,256]{2,1,0:T(8,128)S(1)} %get-tuple-element.8), channel_id=1, source_target_pairs={{2,0},{3,1},{6,4},{7,5},{10,8},{11,9},{14,12},{15,13},{18,16},{19,... | collective-permute-start | bytes 786440 | tf_op jit(solution)/shard_map/ppermute | solution.py:23
  13.9 0.1 reshape.208
  14.0 0.7 iota_compare_fusion.1
  14.7 0.7 add_subtract_fusion
  15.3 0.7 select_reduce_fusion.1
  16.1 0.8 select_reduce_fusion
  16.9 0.1 subtract_multiply_fusion
  16.9 0.5 fusion.10
  17.5 0.6 collective-permute-done
  18.1 4.1 %collective-permute-done.1 = f32[16,16,256]{2,1,0:T(8,128)S(1)} collective-permute-done((f32[16,16,256]{2,1,0:T(8,128)S(1)}, f32[16,16,256]{2,1,0:T(8,128)S(1)}, u32[]{:S(2)}, u32[]{:S(2)}) %collective-permute-start.1) | collective-permute-done | bytes 262176 | tf_op jit(solution)/shard_map/ppermute | solution.py:23
  22.2 0.0 copy-done
  22.2 0.1 pad_maximum_fusion.1
  22.4 1.4 %copy.12 = f32[14,8,16,256]{3,1,2,0:T(8,128)S(1)} copy(f32[14,8,16,256]{3,2,1,0:T(8,128)S(1)} %bitcast.20) | data formatting | bytes 3670016
  23.8 3.2 %fusion.36 = f32[128,4096]{1,0:T(8,128)} fusion(f32[128,112]{1,0:T(8,128)S(1)} %fusion.10, f32[112,4096]{1,0:T(8,128)S(1)} %bitcast.21), kind=kOutput, calls=%fused_computation.66 | convolution fusion | flops 704643072 | bytes 3989504 | tf_op jit(solution)/shard_map/dot_general | solution.py:66
  26.9 0.0 reduce-scatter.2.cloned.1.call-update
  27.0 32.3 %reduce-scatter.2.cloned.1.call-done = f32[64,4096]{1,0:T(8,128)} async-done(((f32[128,4096]{1,0:T(8,128)}), f32[64,4096]{1,0:T(8,128)}) %reduce-scatter.2.cloned.1.call-update) | async-done | bytes 1048592 | tf_op jit(solution)/shard_map/reduce_scatter | solution.py:69
  59.3 0.0 copy-start.2
  59.3 0.0 copy-start.1
  59.3 2.5 %copy.13 = f32[8,8,16,256]{3,2,1,0:T(8,128)} copy(f32[8,8,16,256]{3,1,2,0:T(8,128)} %bitcast.23) | data formatting | bytes 2097152
  61.8 4.6 %all-to-all-start = ((f32[64,16,256]{2,1,0:T(8,128)}), f32[64,16,256]{2,1,0:T(8,128)S(1)}, u32[]{:S(2)}, u32[]{:S(2)}) async-start(f32[64,16,256]{2,1,0:T(8,128)} %bitcast.12), calls=%async_computation.1 | async-start | bytes 2097152 | tf_op jit(solution)/shard_map/all_to_all | solution.py:71
  66.4 0.0 copy-done.2
  66.4 0.6 dynamic-slice
  67.6 0.0 copy-done.1
  67.6 0.2 dynamic-update-slice
  67.8 21.8 %all-reduce.1 = f32[64]{0:T(128)S(1)} all-reduce(f32[64]{0:T(128)S(1)} %dynamic-update-slice), channel_id=1, replica_groups=mesh['blocks'=2,'space'=4,'tm'=2,'span'=2] {'space'}, use_global_device_ids=true, to_apply=%add.1 | all-reduce | flops 64 | bytes 512
  89.6 2.7 %all-to-all-done = f32[64,16,256]{2,1,0:T(8,128)S(1)} async-done(((f32[64,16,256]{2,1,0:T(8,128)}), f32[64,16,256]{2,1,0:T(8,128)S(1)}, u32[]{:S(2)}, u32[]{:S(2)}) %all-to-all-start) | async-done | bytes 1048608 | tf_op jit(solution)/shard_map/all_to_all | solution.py:71
  92.3 0.1 copy.10
  92.4 0.2 fusion.35
  92.6 0.1 collective-permute-start.2
  92.7 0.5 collective-permute-start.3
  93.2 1.4 %collective-permute-done.2 = f32[16,64,1]{2,1,0:T(8,128)S(1)} collective-permute-done((f32[16,64,1]{2,1,0:T(8,128)S(1)}, f32[16,64,1]{2,1,0:T(8,128)S(1)}, u32[]{:S(2)}, u32[]{:S(2)}) %collective-permute-start.2) | collective-permute-done | bytes 4128 | tf_op jit(solution)/shard_map/ppermute | solution.py:23
  94.6 0.7 collective-permute-done.3
  95.4 0.8 fusion.2
  96.2 1.5 %pad_maximum_fusion = f32[16,2,64,256]{3,2,1,0:T(8,128)} fusion(f32[16,1,64,256]{3,2,1,0:T(8,128)S(1)} %get-tuple-element.10, f32[16,1,64,256]{3,2,1,0:T(8,128)S(1)} %get-tuple-element.9), kind=kLoop, calls=%fused_computation | loop fusion | flops 524288 | bytes 4194304 | tf_op jit(solution)/shard_map/stack | solution.py:77
  (6 shorter events, 0.1 us)
Async XLA Ops:
  6.5 15.7 %copy-start = (f32[80,16,256]{2,1,0:T(8,128)S(1)}, f32[80,16,256]{2,1,0:T(8,128)}, u32[]{:S(2)}) copy-start(f32[80,16,256]{2,1,0:T(8,128)} %param.6) | copy-start | bytes 3932164
  6.5 52.7 %reduce-scatter.2.cloned.1.call-start = ((), (), s32[]{:S(2)}) async-start(), calls=%async_computation.2 | async-start | bytes 3145728 | tf_op jit(solution)/shard_map/reduce_scatter | solution.py:69
  7.7 10.4 %collective-permute-start = (f32[16,16,256]{2,1,0:T(8,128)S(1)}, f32[16,16,256]{2,1,0:T(8,128)S(1)}, u32[]{:S(2)}, u32[]{:S(2)}) collective-permute-start(f32[16,16,256]{2,1,0:T(8,128)S(1)} %get-tuple-element.7), channel_id=1, source_target_pairs={{0,2},{1,3},{4,6},{5,7},{8,10},{9,11},{12,14},{13,15},{16,18},{17,... | collective-permute-start | bytes 786440 | tf_op jit(solution)/shard_map/ppermute | solution.py:21
  12.6 9.7 %collective-permute-start.1 = (f32[16,16,256]{2,1,0:T(8,128)S(1)}, f32[16,16,256]{2,1,0:T(8,128)S(1)}, u32[]{:S(2)}, u32[]{:S(2)}) collective-permute-start(f32[16,16,256]{2,1,0:T(8,128)S(1)} %get-tuple-element.8), channel_id=1, source_target_pairs={{2,0},{3,1},{6,4},{7,5},{10,8},{11,9},{14,12},{15,13},{18,16},{19,... | collective-permute-start | bytes 786440 | tf_op jit(solution)/shard_map/ppermute | solution.py:23
  59.3 7.1 %copy-start.2 = (u32[32]{0:T(128)S(1)}, u32[32]{0:T(128)}, u32[]{:S(2)}) copy-start(u32[32]{0:T(128)} %constant.95) | copy-start | bytes 388
  59.3 8.3 %copy-start.1 = (f32[16]{0:T(128)S(1)}, f32[16]{0:T(128)}, u32[]{:S(2)}) copy-start(f32[16]{0:T(128)} %param.11) | copy-start | bytes 196
  61.8 30.5 %all-to-all-start = ((f32[64,16,256]{2,1,0:T(8,128)}), f32[64,16,256]{2,1,0:T(8,128)S(1)}, u32[]{:S(2)}, u32[]{:S(2)}) async-start(f32[64,16,256]{2,1,0:T(8,128)} %bitcast.12), calls=%async_computation.1 | async-start | bytes 2097152 | tf_op jit(solution)/shard_map/all_to_all | solution.py:71
  92.6 2.0 %collective-permute-start.2 = (f32[16,64,1]{2,1,0:T(8,128)S(1)}, f32[16,64,1]{2,1,0:T(8,128)S(1)}, u32[]{:S(2)}, u32[]{:S(2)}) collective-permute-start(f32[16,64,1]{2,1,0:T(8,128)S(1)} %get-tuple-element.11), channel_id=1, source_target_pairs={{1,0},{0,1},{3,2},{2,3},{5,4},{4,5},{7,6},{6,7},{9,8},{8,9},{11,10... | collective-permute-start | bytes 12296 | tf_op jit(solution)/shard_map/ppermute | solution.py:23
  92.7 2.6 %collective-permute-start.3 = (f32[16,64,1]{2,1,0:T(8,128)S(1)}, f32[16,64,1]{2,1,0:T(8,128)S(1)}, u32[]{:S(2)}, u32[]{:S(2)}) collective-permute-start(f32[16,64,1]{2,1,0:T(8,128)S(1)} %get-tuple-element.12), channel_id=1, source_target_pairs={{0,1},{1,0},{2,3},{3,2},{4,5},{5,4},{6,7},{7,6},{8,9},{9,8},{10,11... | collective-permute-start | bytes 12296 | tf_op jit(solution)/shard_map/ppermute | solution.py:21
Sparse Core Ops, SparseCore 0:
  27.1 32.1 reduce-scatter.1
where the time goes:
time: 105 us
  waiting for transfers between devices  42 us (40%)
  blocking collectives  21.8 us (21%)
  between operations  14.1 us (13%)
  starting transfers between devices  11.3 us (11%)
  local copies, waits for them, and re-layouts  6.28 us (6%)
  other arithmetic  5.39 us (5%)
  matrix products  3.72 us (4%)
    reduce_scatter x1, waiting for transfers between devices, shards(): summed = lax.psum_scatter(partial, 'tm', scatter_dimension=0, tiled=True)  32.3 us
    unnamed x1, blocking collectives  21.8 us
    ppermute x2, waiting for transfers between devices, extended(): lax.ppermute(head, axis, [((i + 1) % count, i) for i in range(ends)])  5.52 us
    ppermute x2, starting transfers between devices, extended(): lax.ppermute(tail, axis, [(i, (i + 1) % count) for i in range(ends)])  5.36 us
    unnamed x11, local copies, waits for them, and re-layouts  4.74 us
    all_to_all x1, starting transfers between devices, shards(): lax.all_to_all(summed, 'space', split_axis=0, concat_axis=1, tiled=True)  4.59 us
    dot_general x1, matrix products, shards(): jnp.dot(combined, reach.reshape(reach_len, rows_dev * span_cells), precis...  3.18 us
    all_to_all x1, waiting for transfers between devices, shards(): lax.all_to_all(summed, 'space', split_axis=0, concat_axis=1, tiled=True)  2.73 us
  transfers between devices with their start and end apart: 6, of which 6 were waited for; matrix products, arithmetic and copies ran while one was open for 4% of the time, Pallas kernels for 0%

commit v1 on v0

--- a/solution.py
+++ b/solution.py
@@ -68,7 +68,18 @@
     )
     summed = lax.psum_scatter(partial, "tm", scatter_dimension=0, tiled=True)
     summed = summed.reshape(n_space * own, rows_dev, span_cells)
-    fields = lax.all_to_all(summed, "space", split_axis=0, concat_axis=1, tiled=True)
+    ways, here = (lax.axis_size("space"), lax.axis_index("space"))
+    width_2 = summed.shape[0] // ways
+    lengths = list(summed.shape)
+    lengths[0] = width_2
+    height = lengths[1]
+    lengths[1] = height * ways
+    fields = jnp.zeros(lengths, summed.dtype)
+    for mask in range(ways):
+        part = lax.dynamic_slice_in_dim(summed, (here ^ mask) * width_2, width_2, axis=0)
+        if mask:
+            part = lax.ppermute(part, "space", [(d, d ^ mask) for d in range(ways)])
+        fields = lax.dynamic_update_slice_in_dim(fields, part, (here ^ mask) * height, axis=1)
     metric = lax.all_gather(row_metric, "space", tiled=True)
     row_padded = jnp.pad(fields, ((0, 0), (1, 1), (0, 0)))
     along_rows = 0.5 * metric[None, :, None] * (row_padded[:, 2:, :] - row_padded[:, :-2, :])

time: 105 us -> 101 us (0.962)
  the two profiles are of different devices: /device:TPU:0 before, /device:TPU:17 now
where the time goes in v1:
time: 101 us
  waiting for transfers between devices  39.4 us (39%)
  blocking collectives  22.5 us (22%)
  between operations  14.2 us (14%)
  starting transfers between devices  9.88 us (10%)
  local copies, waits for them, and re-layouts  5.47 us (5%)
  other arithmetic  5.39 us (5%)
  matrix products  3.72 us (4%)
    reduce_scatter x1, waiting for transfers between devices, shards(): summed = lax.psum_scatter(partial, 'tm', scatter_dimension=0, tiled=True)  33.3 us
    unnamed x1, blocking collectives  22.5 us
    ppermute x2, waiting for transfers between devices, extended(): lax.ppermute(head, axis, [((i + 1) % count, i) for i in range(ends)])  5.26 us
    ppermute x2, starting transfers between devices, extended(): lax.ppermute(head, axis, [((i + 1) % count, i) for i in range(ends)])  3.96 us
    unnamed x11, local copies, waits for them, and re-layouts  3.75 us
    ppermute x2, starting transfers between devices, extended(): lax.ppermute(tail, axis, [(i, (i + 1) % count) for i in range(ends)])  3.21 us
    dot_general x1, matrix products, shards(): jnp.dot(combined, reach.reshape(reach_len, rows_dev * span_cells), precis...  3.18 us
    ppermute x3, starting transfers between devices, shards(): part = lax.ppermute(part, 'space', [(d, d ^ mask) for d in range(ways)])  2.71 us
  transfers between devices with their start and end apart: 8, of which 5 were waited for; matrix products, arithmetic and copies ran while one was open for 4% of the time, Pallas kernels for 0%

profile of v1, /device:TPU:17, one launch (start us, length us, event | category | flops | bytes accessed | tf_op | source)
XLA Modules:
  0.0 100.5 jit_solution(18077622467783512832)
XLA Ops:
  6.5 0.0 copy-start
  6.5 0.0 reduce-scatter.2.cloned.1.call-start
  6.5 1.2 %fusion.34 = (f32[16,16,256]{2,1,0:T(8,128)S(1)}, f32[16,16,256]{2,1,0:T(8,128)S(1)}) fusion(f32[80,16,256]{2,1,0:T(8,128)} %param.6), kind=kLoop, calls=%fused_computation.71 | loop fusion | bytes 1048576 | tf_op jit(solution)/shard_map/slice | solution.py:18
  7.7 3.1 %collective-permute-start = (f32[16,16,256]{2,1,0:T(8,128)S(1)}, f32[16,16,256]{2,1,0:T(8,128)S(1)}, u32[]{:S(2)}, u32[]{:S(2)}) collective-permute-start(f32[16,16,256]{2,1,0:T(8,128)S(1)} %get-tuple-element.7), channel_id=1, source_target_pairs={{0,2},{1,3},{4,6},{5,7},{8,10},{9,11},{12,14},{13,15},{16,18},{17,... | collective-permute-start | bytes 786440 | tf_op jit(solution)/shard_map/ppermute | solution.py:21
  10.8 1.3 %collective-permute-start.1 = (f32[16,16,256]{2,1,0:T(8,128)S(1)}, f32[16,16,256]{2,1,0:T(8,128)S(1)}, u32[]{:S(2)}, u32[]{:S(2)}) collective-permute-start(f32[16,16,256]{2,1,0:T(8,128)S(1)} %get-tuple-element.8), channel_id=1, source_target_pairs={{2,0},{3,1},{6,4},{7,5},{10,8},{11,9},{14,12},{15,13},{18,16},{19,... | collective-permute-start | bytes 786440 | tf_op jit(solution)/shard_map/ppermute | solution.py:23
  12.2 0.1 reshape.208
  12.3 0.7 iota_compare_fusion.1
  13.0 0.7 select_reduce_fusion.1
  13.7 0.7 add_subtract_fusion
  14.4 0.8 select_reduce_fusion
  15.1 0.1 subtract_multiply_fusion
  15.2 0.5 fusion.10
  15.7 0.1 collective-permute-done
  15.8 3.8 %collective-permute-done.1 = f32[16,16,256]{2,1,0:T(8,128)S(1)} collective-permute-done((f32[16,16,256]{2,1,0:T(8,128)S(1)}, f32[16,16,256]{2,1,0:T(8,128)S(1)}, u32[]{:S(2)}, u32[]{:S(2)}) %collective-permute-start.1) | collective-permute-done | bytes 262176 | tf_op jit(solution)/shard_map/ppermute | solution.py:23
  19.6 0.0 copy-done
  19.6 0.1 pad_maximum_fusion.1
  19.8 1.4 %copy.10 = f32[14,8,16,256]{3,1,2,0:T(8,128)S(1)} copy(f32[14,8,16,256]{3,2,1,0:T(8,128)S(1)} %bitcast.14) | data formatting | bytes 3670016
  21.1 3.2 %fusion.36 = f32[128,4096]{1,0:T(8,128)} fusion(f32[128,112]{1,0:T(8,128)S(1)} %fusion.10, f32[112,4096]{1,0:T(8,128)S(1)} %bitcast.15), kind=kOutput, calls=%fused_computation.73 | convolution fusion | flops 704643072 | bytes 3989504 | tf_op jit(solution)/shard_map/dot_general | solution.py:66
  24.3 0.0 reduce-scatter.2.cloned.1.call-update
  24.4 33.3 %reduce-scatter.2.cloned.1.call-done = f32[64,4096]{1,0:T(8,128)} async-done(((f32[128,4096]{1,0:T(8,128)}), f32[64,4096]{1,0:T(8,128)}) %reduce-scatter.2.cloned.1.call-update) | async-done | bytes 1048592 | tf_op jit(solution)/shard_map/reduce_scatter | solution.py:69
  57.7 1.5 %copy.11 = f32[8,8,16,256]{3,2,1,0:T(8,128)S(1)} copy(f32[8,8,16,256]{3,1,2,0:T(8,128)} %bitcast.17) | data formatting | bytes 2097152
  59.2 0.0 copy-start.2
  59.2 0.0 copy-start.1
  59.2 0.1 broadcast_in_dim.31
  59.3 0.1 constant_dynamic-slice_fusion.2
  59.4 1.2 %collective-permute-start.2 = (f32[16,16,256]{2,1,0:T(8,128)S(1)}, f32[16,16,256]{2,1,0:T(8,128)S(1)}, u32[]{:S(2)}, u32[]{:S(2)}) collective-permute-start(f32[16,16,256]{2,1,0:T(8,128)S(1)} %get-tuple-element.15), channel_id=1, source_target_pairs={{0,4},{4,0},{8,12},{12,8},{1,5},{5,1},{9,13},{13,9},{2,6},{6,2},{1... | collective-permute-start | bytes 786440 | tf_op jit(solution)/shard_map/ppermute | solution.py:81
  60.7 0.3 collective-permute-start.3
  60.9 1.2 %collective-permute-start.4 = (f32[16,16,256]{2,1,0:T(8,128)S(1)}, f32[16,16,256]{2,1,0:T(8,128)S(1)}, u32[]{:S(2)}, u32[]{:S(2)}) collective-permute-start(f32[16,16,256]{2,1,0:T(8,128)S(1)} %get-tuple-element.13), channel_id=1, source_target_pairs={{0,12},{4,8},{8,4},{12,0},{1,13},{5,9},{9,5},{13,1},{2,14},{6,10},... | collective-permute-start | bytes 786440 | tf_op jit(solution)/shard_map/ppermute | solution.py:81
  62.1 0.0 copy-done.2
  62.1 0.6 dynamic-slice
  63.4 0.0 copy-done.1
  63.4 0.2 dynamic-update-slice
  63.6 22.5 %all-reduce.1 = f32[64]{0:T(128)S(1)} all-reduce(f32[64]{0:T(128)S(1)} %dynamic-update-slice), channel_id=1, replica_groups=mesh['blocks'=2,'space'=4,'tm'=2,'span'=2] {'space'}, use_global_device_ids=true, to_apply=%add.1 | all-reduce | flops 64 | bytes 512
  86.1 0.0 collective-permute-done.2
  86.1 0.0 collective-permute-done.3
  86.2 0.0 collective-permute-done.4
  86.2 0.2 fusion.35
  86.4 2.7 %collective-permute-start.5 = (f32[16,64,1]{2,1,0:T(8,128)S(1)}, f32[16,64,1]{2,1,0:T(8,128)S(1)}, u32[]{:S(2)}, u32[]{:S(2)}) collective-permute-start(f32[16,64,1]{2,1,0:T(8,128)S(1)} %get-tuple-element.11), channel_id=1, source_target_pairs={{1,0},{0,1},{3,2},{2,3},{5,4},{4,5},{7,6},{6,7},{9,8},{8,9},{11,10... | collective-permute-start | bytes 12296 | tf_op jit(solution)/shard_map/ppermute | solution.py:23
  89.1 0.1 collective-permute-start.6
  89.2 1.5 %collective-permute-done.5 = f32[16,64,1]{2,1,0:T(8,128)S(1)} collective-permute-done((f32[16,64,1]{2,1,0:T(8,128)S(1)}, f32[16,64,1]{2,1,0:T(8,128)S(1)}, u32[]{:S(2)}, u32[]{:S(2)}) %collective-permute-start.5) | collective-permute-done | bytes 4128 | tf_op jit(solution)/shard_map/ppermute | solution.py:23
  90.6 0.7 collective-permute-done.6
  91.4 0.8 fusion.2
  92.2 1.5 %pad_maximum_fusion = f32[16,2,64,256]{3,2,1,0:T(8,128)} fusion(f32[16,1,64,256]{3,2,1,0:T(8,128)S(1)} %get-tuple-element.10, f32[16,1,64,256]{3,2,1,0:T(8,128)S(1)} %get-tuple-element.9), kind=kLoop, calls=%fused_computation | loop fusion | flops 524288 | bytes 4194304 | tf_op jit(solution)/shard_map/stack | solution.py:88
  (9 shorter events, 0.1 us)
Async XLA Ops:
  6.5 13.1 %copy-start = (f32[80,16,256]{2,1,0:T(8,128)S(1)}, f32[80,16,256]{2,1,0:T(8,128)}, u32[]{:S(2)}) copy-start(f32[80,16,256]{2,1,0:T(8,128)} %param.6) | copy-start | bytes 3932164
  6.5 51.1 %reduce-scatter.2.cloned.1.call-start = ((), (), s32[]{:S(2)}) async-start(), calls=%async_computation.1 | async-start | bytes 3145728 | tf_op jit(solution)/shard_map/reduce_scatter | solution.py:69
  7.7 8.1 %collective-permute-start = (f32[16,16,256]{2,1,0:T(8,128)S(1)}, f32[16,16,256]{2,1,0:T(8,128)S(1)}, u32[]{:S(2)}, u32[]{:S(2)}) collective-permute-start(f32[16,16,256]{2,1,0:T(8,128)S(1)} %get-tuple-element.7), channel_id=1, source_target_pairs={{0,2},{1,3},{4,6},{5,7},{8,10},{9,11},{12,14},{13,15},{16,18},{17,... | collective-permute-start | bytes 786440 | tf_op jit(solution)/shard_map/ppermute | solution.py:21
  10.8 8.8 %collective-permute-start.1 = (f32[16,16,256]{2,1,0:T(8,128)S(1)}, f32[16,16,256]{2,1,0:T(8,128)S(1)}, u32[]{:S(2)}, u32[]{:S(2)}) collective-permute-start(f32[16,16,256]{2,1,0:T(8,128)S(1)} %get-tuple-element.8), channel_id=1, source_target_pairs={{2,0},{3,1},{6,4},{7,5},{10,8},{11,9},{14,12},{15,13},{18,16},{19,... | collective-permute-start | bytes 786440 | tf_op jit(solution)/shard_map/ppermute | solution.py:23
  59.2 3.0 %copy-start.2 = (u32[32]{0:T(128)S(1)}, u32[32]{0:T(128)}, u32[]{:S(2)}) copy-start(u32[32]{0:T(128)} %constant.105) | copy-start | bytes 388
  59.2 4.2 %copy-start.1 = (f32[16]{0:T(128)S(1)}, f32[16]{0:T(128)}, u32[]{:S(2)}) copy-start(f32[16]{0:T(128)} %param.11) | copy-start | bytes 196
  59.4 26.7 %collective-permute-start.2 = (f32[16,16,256]{2,1,0:T(8,128)S(1)}, f32[16,16,256]{2,1,0:T(8,128)S(1)}, u32[]{:S(2)}, u32[]{:S(2)}) collective-permute-start(f32[16,16,256]{2,1,0:T(8,128)S(1)} %get-tuple-element.15), channel_id=1, source_target_pairs={{0,4},{4,0},{8,12},{12,8},{1,5},{5,1},{9,13},{13,9},{2,6},{6,2},{1... | collective-permute-start | bytes 786440 | tf_op jit(solution)/shard_map/ppermute | solution.py:81
  60.7 25.5 %collective-permute-start.3 = (f32[16,16,256]{2,1,0:T(8,128)S(1)}, f32[16,16,256]{2,1,0:T(8,128)S(1)}, u32[]{:S(2)}, u32[]{:S(2)}) collective-permute-start(f32[16,16,256]{2,1,0:T(8,128)S(1)} %get-tuple-element.14), channel_id=1, source_target_pairs={{0,8},{4,12},{8,0},{12,4},{1,9},{5,13},{9,1},{13,5},{2,10},{6,14},... | collective-permute-start | bytes 786440 | tf_op jit(solution)/shard_map/ppermute | solution.py:81
  60.9 25.2 %collective-permute-start.4 = (f32[16,16,256]{2,1,0:T(8,128)S(1)}, f32[16,16,256]{2,1,0:T(8,128)S(1)}, u32[]{:S(2)}, u32[]{:S(2)}) collective-permute-start(f32[16,16,256]{2,1,0:T(8,128)S(1)} %get-tuple-element.13), channel_id=1, source_target_pairs={{0,12},{4,8},{8,4},{12,0},{1,13},{5,9},{9,5},{13,1},{2,14},{6,10},... | collective-permute-start | bytes 786440 | tf_op jit(solution)/shard_map/ppermute | solution.py:81
  86.4 4.2 %collective-permute-start.5 = (f32[16,64,1]{2,1,0:T(8,128)S(1)}, f32[16,64,1]{2,1,0:T(8,128)S(1)}, u32[]{:S(2)}, u32[]{:S(2)}) collective-permute-start(f32[16,64,1]{2,1,0:T(8,128)S(1)} %get-tuple-element.11), channel_id=1, source_target_pairs={{1,0},{0,1},{3,2},{2,3},{5,4},{4,5},{7,6},{6,7},{9,8},{8,9},{11,10... | collective-permute-start | bytes 12296 | tf_op jit(solution)/shard_map/ppermute | solution.py:23
  89.1 2.3 %collective-permute-start.6 = (f32[16,64,1]{2,1,0:T(8,128)S(1)}, f32[16,64,1]{2,1,0:T(8,128)S(1)}, u32[]{:S(2)}, u32[]{:S(2)}) collective-permute-start(f32[16,64,1]{2,1,0:T(8,128)S(1)} %get-tuple-element.12), channel_id=1, source_target_pairs={{0,1},{1,0},{2,3},{3,2},{4,5},{5,4},{6,7},{7,6},{8,9},{9,8},{10,11... | collective-permute-start | bytes 12296 | tf_op jit(solution)/shard_map/ppermute | solution.py:21
Sparse Core Ops, SparseCore 0:
  24.5 33.1 reduce-scatter.1
